TPU v7x, 32 devices: a whole 2x2x4 slice. The times are simulated.
32 devices in a mesh: groups: 2 (over y), dev: 4 (over z), sub: 4 (over x, core).
Axes of the slice: x: 2, y: 2, z: 4, core: 2. Of those that a mesh axis runs over, the one named last changes fastest.
Arguments:
- query_pre: bfloat16 [8, 16, 256, 128], P('dev', ('groups', 'sub')), parts along dimension 1, may hold values from -0.5390625 to 0.5390625
- key_pre: bfloat16 [8, 16, 256, 128], P('dev', ('groups', 'sub')), parts along dimension 1, may hold values from -0.375 to 0.375
- value_pre: bfloat16 [8, 16, 256, 128], P('dev', ('groups', 'sub')), parts along dimension 1, may hold values from -6 to 6
- decay_pre: float32 [8, 16, 256], P('dev', ('groups', 'sub')), parts along dimension 1, may hold values from -0.75 to 0
- blocks: int32 [16], P('groups'), parts along dimension 0, may hold values from 1 to 2, as said below
- dest_map: int32 [16], P('groups'), parts along dimension 0, may hold values from 0 to 3, as said below
- query_dec: bfloat16 [16, 4, 128, 8], P(('groups', 'dev'), None, 'sub'), parts along dimension 0, may hold values from -0.5390625 to 0.5390625
- key_dec: bfloat16 [16, 4, 128, 8], P(('groups', 'dev'), None, 'sub'), parts along dimension 0, may hold values from -0.375 to 0.375
- value_dec: bfloat16 [16, 4, 8, 128], P(('groups', 'dev')), parts along dimension 0, may hold values from -6 to 6
- decay_dec: float32 [16, 4, 8], P(('groups', 'dev')), parts along dimension 0, may hold values from -0.75 to 0
- gate_dec: bfloat16 [16, 4, 1024], P(('groups', 'dev'), None, 'sub'), parts along dimension 0, may hold values from -6 to 6
- norm_gain: float32 [1024], P('sub'), may hold values from 0.1 to 1.9
Outputs:
- prefill_out: bfloat16 [8, 16, 256, 128], P('dev', ('groups', 'sub')), parts along dimension 1
- decode_out: bfloat16 [16, 4, 1024], P(('groups', 'dev'), None, 'sub'), parts along dimension 0
- final_state: float32 [16, 8, 128, 128], P(('groups', 'dev'), None, 'sub'), parts along dimension 0
There are 2 independent parts, one for each index of `groups`. A program takes and returns all parts, laid end to end along the dimension named above; an argument that names none is the same for every part. Nothing has to cross between parts.
Inputs may be any that keep to these rules, and one draw needn't show every extreme that they name: At least one request has 2 blocks. `dest_map`: every value is named by exactly 2 requests, and the 2 requests of one aligned block of ids name distinct values.
All inputs are finite; a program needn't handle non-finite values.
Results may differ from a plain program's by a relative error of at most 0.001.
Values sent between devices are 32-bit elements; how exact they have to be, the bound alone decides.
A program may use at most 128 MiB of HBM per device.

v0:
```python
import jax
import jax.numpy as jnp
from jax import lax
from jax.sharding import PartitionSpec as P

BLOCK_POSITIONS = 128
MAX_PROMPT_BLOCKS = 2


HIGHEST = lax.Precision.HIGHEST
EPSILON = 1e-06


def prefill_blocks(query_input, key_input, value_input, log_decay, block_count):
    positions = jnp.arange(query_input.shape[2], dtype=jnp.int32)
    valid_mask = (positions[None, :] < block_count[:, None] * BLOCK_POSITIONS).astype(jnp.float32)
    log_decay = log_decay * valid_mask[None]
    key_input = key_input * valid_mask.astype(jnp.bfloat16)[None, :, :, None]
    within = positions[:BLOCK_POSITIONS]
    causal_mask = within[:, None] >= within[None, :]
    head_size = query_input.shape[3]
    carried = jnp.zeros(query_input.shape[:2] + (head_size, head_size), jnp.float32)
    pieces = []
    for block_index in range(MAX_PROMPT_BLOCKS):
        block_start = block_index * BLOCK_POSITIONS
        query_block = query_input[:, :, block_start : block_start + BLOCK_POSITIONS]
        key_block = key_input[:, :, block_start : block_start + BLOCK_POSITIONS]
        value_block = value_input[:, :, block_start : block_start + BLOCK_POSITIONS].astype(
            jnp.float32
        )
        cumulative = jnp.cumsum(
            log_decay[:, :, block_start : block_start + BLOCK_POSITIONS], axis=-1
        )
        offsets = jnp.where(causal_mask, cumulative[..., :, None] - cumulative[..., None, :], 0.0)
        weights = jnp.where(causal_mask, jnp.exp(offsets), 0.0)
        scores = (
            jnp.einsum(
                "hgtd,hgud->hgtu", query_block, key_block, preferred_element_type=jnp.float32
            )
            * weights
        )
        inner_part = jnp.einsum("hgtu,hgud->hgtd", scores, value_block, precision=HIGHEST)
        outer_part = jnp.exp(cumulative)[..., None] * jnp.einsum(
            "hgtd,hgde->hgte", query_block.astype(jnp.float32), carried, precision=HIGHEST
        )
        pieces.append(
            (
                (inner_part + outer_part)
                * valid_mask[None, :, block_start : block_start + BLOCK_POSITIONS, None]
            ).astype(jnp.bfloat16)
        )
        tail_decay = jnp.exp(cumulative[..., -1:] - cumulative)
        carried = jnp.exp(cumulative[..., -1])[..., None, None] * carried + jnp.einsum(
            "hgtd,hgte->hgde",
            key_block.astype(jnp.float32) * tail_decay[..., None],
            value_block,
            precision=HIGHEST,
        )
    return (jnp.concatenate(pieces, axis=2), carried)


def advance(carried_state, inputs):
    query_step, key_step, value_step, decay_step = inputs
    key_cols = jnp.swapaxes(key_step.astype(jnp.float32), 1, 2)
    carried_state = (
        jnp.exp(decay_step)[..., None, None] * carried_state
        + key_cols[..., None] * value_step.astype(jnp.float32)[:, :, None, :]
    )
    reading = jnp.einsum(
        "jhc,jhcd->jhd",
        jnp.swapaxes(query_step.astype(jnp.float32), 1, 2),
        carried_state,
        precision=HIGHEST,
    )
    return (carried_state, reading)


def body(
    query_pre,
    key_pre,
    value_pre,
    decay_pre,
    blocks,
    dest_map,
    query_dec,
    key_dec,
    value_dec,
    decay_dec,
    gate_dec,
    norm_gain,
):
    dev_count = lax.axis_size("dev")
    sub_count = lax.axis_size("sub")
    request_total = dest_map.shape[0]
    group_size = request_total // sub_count
    per_device = request_total // dev_count
    sub_index = lax.axis_index("sub")
    dev_index = lax.axis_index("dev")
    block_count = lax.dynamic_slice_in_dim(blocks, sub_index * group_size, group_size)
    prefill_out, carried = prefill_blocks(query_pre, key_pre, value_pre, decay_pre, block_count)
    request_ids = jnp.arange(request_total, dtype=jnp.int32)
    slot_order = jnp.argsort(dest_map * request_total + request_ids)
    my_slots = lax.dynamic_slice_in_dim(slot_order, dev_index * per_device, per_device)
    head_count = carried.shape[0]
    head_size = carried.shape[3]
    row_count = head_size // sub_count
    split_rows = carried.reshape(head_count, group_size, sub_count, row_count, head_size)
    my_targets = lax.dynamic_slice_in_dim(dest_map, sub_index * group_size, group_size)
    selector = (my_targets[None, :] == jnp.arange(dev_count, dtype=jnp.int32)[:, None]).astype(
        jnp.float32
    )
    outgoing = jnp.einsum("rg,hgsij->rshij", selector, split_rows, precision=HIGHEST)
    outgoing = outgoing.reshape(dev_count * sub_count, head_count, row_count, head_size)
    arrived = lax.all_to_all(outgoing, ("dev", "sub"), split_axis=0, concat_axis=0, tiled=True)
    arrived = arrived.reshape(dev_count, sub_count, head_count, row_count, head_size)
    source_group = my_slots // group_size
    chooser = (source_group[:, None] == jnp.arange(sub_count, dtype=jnp.int32)[None, :]).astype(
        jnp.float32
    )
    received = jnp.einsum("js,dshab->jdhab", chooser, arrived, precision=HIGHEST)
    received = received.reshape(per_device, dev_count * head_count, row_count, head_size)
    final_state, readings = lax.scan(
        advance,
        received,
        (
            jnp.moveaxis(query_dec, 1, 0),
            jnp.moveaxis(key_dec, 1, 0),
            jnp.moveaxis(value_dec, 1, 0),
            jnp.moveaxis(decay_dec, 1, 0),
        ),
    )
    partial_sums = jnp.moveaxis(readings, 0, 1).reshape(per_device, readings.shape[0], -1)
    gate_share = jax.nn.sigmoid(gate_dec.astype(jnp.float32))
    own_share = lax.psum_scatter(partial_sums, "sub", scatter_dimension=2, tiled=True)
    square_sum = lax.psum(jnp.sum(own_share * own_share, axis=-1), "sub")
    inverse_rms = lax.rsqrt(square_sum / (own_share.shape[-1] * sub_count) + EPSILON)[..., None]
    decode_out = (own_share * inverse_rms * norm_gain * gate_share).astype(jnp.bfloat16)
    return (prefill_out, decode_out, final_state)


def solution(mesh):
    placed = (
        P("dev", ("groups", "sub"), None, None),
        P("dev", ("groups", "sub"), None, None),
        P("dev", ("groups", "sub"), None, None),
        P("dev", ("groups", "sub"), None),
        P("groups"),
        P("groups"),
        P(("groups", "dev"), None, "sub", None),
        P(("groups", "dev"), None, "sub", None),
        P(("groups", "dev"), None, None, None),
        P(("groups", "dev"), None, None),
        P(("groups", "dev"), None, "sub"),
        P("sub"),
    )
    return jax.shard_map(
        body,
        mesh=mesh,
        in_specs=placed,
        out_specs=(
            P("dev", ("groups", "sub"), None, None),
            P(("groups", "dev"), None, "sub"),
            P(("groups", "dev"), None, "sub", None),
        ),
        check_vma=False,
    )
```

profile of v0, /device:TPU:0, one launch (start us, length us, event | category | flops | bytes accessed | tf_op | source)
XLA Modules:
  0.0 79.1 jit_solution(11719525150581767050)
XLA Ops:
  7.2 0.0 copy-start.10
  7.2 0.6 copy-done.10
  7.8 0.1 dynamic-slice_multiply_fusion
  7.9 0.1 fusion.47
  8.0 0.5 copy-done.6
  8.5 0.6 reduce_window_sum.18
  9.1 0.2 slice_reduce_fusion
  9.3 0.1 subtract_exponential_fusion
  9.4 0.6 reduce_window_sum.17
  10.0 0.2 slice_reduce_fusion.1
  10.2 0.1 fusion.49
  10.2 0.6 copy-done.11
  10.8 0.1 dynamic_slice.26
  10.9 1.1 %broadcast_multiply_fusion = bf16[2,2,256,128]{3,2,1,0:T(8,128)(2,1)S(1)} fusion(bf16[2,2,256,128]{3,2,1,0:T(8,128)(2,1)} %param.15, bf16[2,256]{1,0:T(2,128)(2,1)S(1)} %get-tuple-element.88), kind=kLoop, calls=%fused_computation.36 | loop fusion | flops 131072 | bytes 525312 | tf_op jit(solution)/shard_map/mul | solution.py:18
  12.0 0.0 copy-done.1
  12.0 0.5 convolution_add_fusion.1
  12.5 0.5 convolution_add_fusion
  13.0 0.8 convolution_bitcast_fusion
  13.8 0.9 %copy.41 = f32[4,4,2,32,128]{4,3,2,1,0:T(8,128)} copy(f32[4,4,2,32,128]{4,0,3,1,2:T(4,128)S(1)} %convolution_bitcast_fusion) | data formatting | bytes 1048576 | tf_op jit(solution)/shard_map/rg,hgsij->rshij/transpose | solution.py:112
  14.7 7.5 %all-to-all-start = ((f32[16,2,32,128]{3,2,1,0:T(8,128)}), f32[16,2,32,128]{3,2,1,0:T(8,128)S(1)}, u32[]{:S(2)}, u32[]{:S(2)}) async-start(f32[16,2,32,128]{3,2,1,0:T(8,128)} %bitcast.20), calls=%async_computation | async-start | bytes 1048576 | tf_op jit(solution)/shard_map/all_to_all | solution.py:114
  22.2 0.0 reduce-scatter.4.cloned.1.call-start
  22.2 0.0 copy-start.4
  22.2 0.0 copy-start.5
  22.3 0.1 broadcast_compare_fusion
  22.4 1.0 %sort.17 = (s32[8]{0:T(128)}, s32[8]{0:T(128)S(1)}) sort(s32[8]{0:T(128)S(1)} %iota_add_fusion, s32[8]{0:T(128)S(1)} %iota.39), dimensions={0}, to_apply=%region_2.3 | sort | flops 24 | bytes 128 | tf_op jit(solution)/shard_map/jit(argsort)/sort | solution.py:102
  23.3 0.0 copy-done.4
  23.4 0.0 copy-done.5
  23.4 0.0 copy-done.2
  23.4 0.0 copy-start.3
  23.4 0.2 fusion.10
  23.6 0.0 copy-start.7
  23.6 0.1 and_select_fusion
  23.7 0.6 copy-done.7
  24.3 0.0 copy-done.3
  24.3 0.2 fusion.11
  24.5 0.4 fusion.32
  24.9 0.4 fusion.27
  25.3 0.3 fusion.12
  25.6 11.0 %all-to-all-done = f32[16,2,32,128]{3,2,1,0:T(8,128)S(1)} async-done(((f32[16,2,32,128]{3,2,1,0:T(8,128)}), f32[16,2,32,128]{3,2,1,0:T(8,128)S(1)}, u32[]{:S(2)}, u32[]{:S(2)}) %all-to-all-start) | async-done | bytes 524320 | tf_op jit(solution)/shard_map/all_to_all | solution.py:114
  36.6 0.3 copy.42
  37.0 0.6 fusion.38
  37.6 2.2 %while.12 = (s32[]{:T(128)}, f32[2,8,32,128]{3,2,1,0:T(8,128)S(1)}, f32[4,2,8,128]{3,2,1,0:T(8,128)S(1)}, f32[4,2,8]{2,1,0:T(2,128)S(1)}, bf16[4,2,32,8]{2,3,1,0...) while((s32[]{:T(128)}, f32[2,8,32,128]{3,2,1,0:T(8,128)S(1)}, ...), condition=%wide.region_4.5_spmd, body=%wide.region_3.4_spmd.sunk | while | flops 985602 | bytes 839985 | solution.py:122
  37.7 0.2 multiply_add_fusion.2
  37.9 0.2 fusion.63
  38.3 0.2 multiply_add_fusion.2
  38.5 0.2 fusion.63
  38.8 0.2 multiply_add_fusion.2
  39.0 0.2 fusion.63
  39.4 0.2 multiply_add_fusion.2
  39.6 0.2 fusion.63
  39.8 0.0 copy-start
  39.8 0.5 copy.62
  40.3 0.2 copy-done
  40.5 1.4 %reshape.124 = f32[1024,8]{1,0:T(8,128)} reshape(f32[1024,2,4]{2,1,0:T(2,128)S(1)} %bitcast.95) | data formatting | bytes 65536
  41.9 0.0 reduce-scatter.4.cloned.1.call-update
  41.9 0.2 fusion.13
  42.2 21.0 %reduce-scatter.4.cloned.1.call-done = f32[256,8]{1,0:T(8,128)} async-done(((f32[1024,8]{1,0:T(8,128)}), f32[256,8]{1,0:T(8,128)}) %reduce-scatter.4.cloned.1.call-update) | async-done | bytes 8208
  63.2 1.1 %reshape.125 = f32[256,2,4]{2,1,0:T(2,128)S(1)} reshape(f32[256,8]{1,0:T(8,128)} %reduce-scatter.4.cloned.1.call-done) | data formatting | bytes 16384
  64.3 0.1 copy.60
  64.4 0.1 multiply_reduce_fusion
  64.5 0.7 pad_maximum_fusion
  65.2 5.7 %psum.7 = f32[2,4]{1,0:T(2,128)S(1)} all-reduce(f32[2,4]{1,0:T(2,128)S(1)} %multiply_reduce_fusion), channel_id=1, replica_groups=mesh['groups'=2,'dev'=4,'sub'=4] {'sub'}, use_global_device_ids=true, to_apply=%region_7.8 | all-reduce | flops 8 | bytes 64 | tf_op jit(solution)/shard_map/psum | solution.py:135
  71.0 0.7 copy-done.9
  71.6 0.7 fusion.36
  (42 shorter events, 0.3 us)
Async XLA Ops:
  7.2 0.7 copy-start.10
  7.8 0.7 copy-start.6
  10.2 0.7 copy-start.11
  10.9 1.1 %copy-start.1 = (bf16[2,2,256,128]{3,2,1,0:T(8,128)(2,1)S(1)}, bf16[2,2,256,128]{3,2,1,0:T(8,128)(2,1)}, u32[]{:S(2)}) copy-start(bf16[2,2,256,128]{3,2,1,0:T(8,128)(2,1)} %param.16) | copy-start | bytes 786436
  14.7 8.7 %copy-start.2 = (bf16[2,2,256,128]{3,2,1,0:T(8,128)(2,1)S(1)}, bf16[2,2,256,128]{3,2,1,0:T(8,128)(2,1)}, u32[]{:S(2)}) copy-start(bf16[2,2,256,128]{3,2,1,0:T(8,128)(2,1)} %param.14) | copy-start | bytes 786436
  14.7 22.0 %all-to-all-start = ((f32[16,2,32,128]{3,2,1,0:T(8,128)}), f32[16,2,32,128]{3,2,1,0:T(8,128)S(1)}, u32[]{:S(2)}, u32[]{:S(2)}) async-start(f32[16,2,32,128]{3,2,1,0:T(8,128)} %bitcast.20), calls=%async_computation | async-start | bytes 1048576 | tf_op jit(solution)/shard_map/all_to_all | solution.py:114
  22.2 41.0 %reduce-scatter.4.cloned.1.call-start = ((), (), s32[]{:S(2)}) async-start(), calls=%async_computation.2 | async-start | bytes 655360
  22.2 1.1 %copy-start.4 = (bf16[2,4,32,8]{2,3,1,0:T(8,128)(2,1)S(1)}, bf16[2,4,32,8]{2,3,1,0:T(8,128)(2,1)}, u32[]{:S(2)}) copy-start(bf16[2,4,32,8]{2,3,1,0:T(8,128)(2,1)} %param.20) | copy-start | bytes 12292
  22.2 1.1 %copy-start.5 = (bf16[2,4,32,8]{2,3,1,0:T(8,128)(2,1)S(1)}, bf16[2,4,32,8]{2,3,1,0:T(8,128)(2,1)}, u32[]{:S(2)}) copy-start(bf16[2,4,32,8]{2,3,1,0:T(8,128)(2,1)} %param.21) | copy-start | bytes 12292
  23.4 0.9 %copy-start.3 = (bf16[2,4,8,128]{3,2,1,0:T(8,128)(2,1)S(1)}, bf16[2,4,8,128]{3,2,1,0:T(8,128)(2,1)}, u32[]{:S(2)}) copy-start(bf16[2,4,8,128]{3,2,1,0:T(8,128)(2,1)} %param.22) | copy-start | bytes 49156
  23.6 0.7 copy-start.7
  39.8 0.7 copy-start
  64.5 6.5 %copy-start.8 = (bf16[2,4,256]{2,1,0:T(4,128)(2,1)S(1)}, bf16[2,4,256]{2,1,0:T(4,128)(2,1)}, u32[]{:S(2)}) copy-start(bf16[2,4,256]{2,1,0:T(4,128)(2,1)} %param.24) | copy-start | bytes 12292
  71.0 0.7 copy-start.9
Sparse Core Ops, SparseCore 0:
  42.1 21.0 reduce-scatter.3
where the time goes:
time: 79.5 us; the launch traced here: 79.1 us
  waiting for transfers between devices  32 us (40%)
  between operations  14.3 us (18%)
  local copies, waits for them, and re-layouts  8.12 us (10%)
  starting transfers between devices  7.53 us (9%)
  other arithmetic  6.12 us (8%)
  blocking collectives  5.73 us (7%)
  matrix products  5.07 us (6%)
    unnamed x2, waiting for transfers between devices  21 us
    all_to_all x1, waiting for transfers between devices, body(): lax.all_to_all(outgoing, ('dev', 'sub'), split_axis=0, concat_axis=0, til...  11 us
    all_to_all x1, starting transfers between devices, body(): lax.all_to_all(outgoing, ('dev', 'sub'), split_axis=0, concat_axis=0, til...  7.49 us
    unnamed x30, local copies, waits for them, and re-layouts  6.36 us
    psum x1, blocking collectives, body(): square_sum = lax.psum(jnp.sum(own_share * own_share, axis=-1), 'sub')  5.73 us
  transfers between devices with their start and end apart: 2, of which 2 were waited for; matrix products, arithmetic and copies ran while one was open for 4% of the time, Pallas kernels for 0%

commit v1 on v0

v1 whole, which is shorter than its diff:
```python
import functools

import jax
import jax.numpy as jnp
from jax import lax
from jax.experimental import pallas as pl
from jax.experimental.pallas import tpu as pltpu
from jax.sharding import PartitionSpec as P

BLOCK = 128
EPSILON = 1e-06
HIGHEST = lax.Precision.HIGHEST
F32 = jnp.float32
BF16 = jnp.bfloat16
CHUNK = 8


def each(low, high, step):
    if high - low <= 8:
        for i in range(low, high):
            step(i)
    else:

        def turn(i, carry):
            step(i)
            return carry

        lax.fori_loop(low, high, turn, 0)


def dot(a, b, contract, precision=None):
    return lax.dot_general(
        a, b, (contract, ((), ())), precision=precision, preferred_element_type=F32
    )


NN = ((1,), (0,))
NT = ((1,), (1,))
TN = ((0,), (0,))


def split(x):
    high = x.astype(BF16)
    return high, (x - high.astype(F32)).astype(BF16)


def iota(shape, dimension):
    return lax.broadcasted_iota(jnp.int32, shape, dimension)


def kernel(
    n_dev,
    n_sub,
    q_ref,
    k_ref,
    v_ref,
    d_ref,
    blocks_ref,
    dest_ref,
    qd_ref,
    kd_ref,
    vd_ref,
    dd_ref,
    gate_ref,
    gain_ref,
    out_hbm,
    dec_ref,
    fin_hbm,
    sbuf,
    bbuf,
    rbuf,
    fsbuf,
    pbuf,
    dbuf,
    qbuf,
    ebuf,
    ybuf,
    ysum,
    send_a,
    recv_a,
    send_b,
    recv_b,
    send_y,
    recv_y,
    local,
    *mids,
):
    heads, group, length, width = q_ref.shape
    prompt_blocks = length // BLOCK
    slots, steps, rows, all_heads = qd_ref.shape
    requests = dest_ref.shape[0]
    chunks = all_heads // CHUNK
    lanes = CHUNK * rows
    sub = lax.axis_index("sub")
    dev = lax.axis_index("dev")

    barrier = pltpu.get_barrier_semaphore()

    def greet_sub(i):
        pl.semaphore_signal(
            barrier,
            inc=1,
            device_id={"sub": lax.rem(sub + i, n_sub)},
            device_id_type=pl.DeviceIdType.MESH,
        )

    def greet_dev(i):
        pl.semaphore_signal(
            barrier,
            inc=1,
            device_id={"dev": lax.rem(dev + i, n_dev)},
            device_id_type=pl.DeviceIdType.MESH,
        )

    each(1, n_sub, greet_sub)
    each(1, n_dev, greet_dev)

    lower = iota((BLOCK, BLOCK), 0) >= iota((BLOCK, BLOCK), 1)
    diagonal = iota((BLOCK, BLOCK), 0) == iota((BLOCK, BLOCK), 1)

    def live(g, b):
        return jnp.where(blocks_ref[sub * group + g] > b, 1.0, 0.0).astype(F32)

    def cumulative(hd, g, b):
        row = dbuf[hd, g, :, b * BLOCK : (b + 1) * BLOCK] * live(g, b)
        return jnp.sum(
            jnp.where(lower, jnp.broadcast_to(row, (BLOCK, BLOCK)), 0.0),
            axis=1,
            keepdims=True,
        )

    def state(hd, g):
        after = None
        weighted = []
        for b in reversed(range(prompt_blocks)):
            col = cumulative(hd, g, b)
            last = col[BLOCK - 1 :, :]
            tail = last - col if after is None else last - col + after
            after = last if after is None else after + last
            part = v_ref[hd, g, b * BLOCK : (b + 1) * BLOCK, :].astype(F32)
            weighted.append(part * (jnp.exp(tail) * live(g, b)))
        high, low = split(jnp.concatenate(weighted[::-1], axis=0))
        both = dot(k_ref[hd, g], jnp.concatenate([high, low], axis=1), TN)
        total = both[:, :width] + both[:, width:]
        for s in range(n_sub):
            sbuf[hd, s, g] = total[s * rows : (s + 1) * rows, :]

    def output(hd, g):
        cols = [cumulative(hd, g, b) for b in range(prompt_blocks)]
        flat = [
            jnp.sum(
                jnp.where(diagonal, jnp.broadcast_to(c, (BLOCK, BLOCK)), 0.0),
                axis=0,
                keepdims=True,
            )
            for c in cols
        ]
        for b in range(prompt_blocks):
            q = q_ref[hd, g, b * BLOCK : (b + 1) * BLOCK, :]
            total = None
            before = None
            for a in reversed(range(b + 1)):
                k = k_ref[hd, g, a * BLOCK : (a + 1) * BLOCK, :]
                v = v_ref[hd, g, a * BLOCK : (a + 1) * BLOCK, :]
                if a == b:
                    weights = jnp.where(
                        lower, jnp.exp(jnp.where(lower, cols[b] - flat[a], 0.0)), 0.0
                    )
                else:
                    gap = cols[a][BLOCK - 1 :, :] - flat[a]
                    if before is not None:
                        gap = gap + before
                    weights = jnp.exp(cols[b] + gap)
                    ending = cols[a][BLOCK - 1 :, :]
                    before = ending if before is None else before + ending
                high, low = split(dot(q, k, NT) * weights)
                term = dot(
                    jnp.concatenate([high, low], axis=1),
                    jnp.concatenate([v, v], axis=0),
                    NN,
                )
                total = term if total is None else total + term
            pbuf[hd, g, b * BLOCK : (b + 1) * BLOCK, :] = (total * live(g, b)).astype(
                BF16
            )

    def copy_a(hd, i):
        to = lax.rem(sub + i, n_sub)
        return pltpu.make_async_remote_copy(
            src_ref=sbuf.at[hd, to],
            dst_ref=mids[hd].at[pl.ds(sub * group, group)],
            send_sem=send_a.at[hd, i],
            recv_sem=recv_a.at[hd, i],
            device_id={"sub": to},
            device_id_type=pl.DeviceIdType.MESH,
        )

    def copy_b(hd, i):
        to = lax.rem(dev + i, n_dev)
        return pltpu.make_async_remote_copy(
            src_ref=bbuf.at[hd, i],
            dst_ref=rbuf.at[dev, hd],
            send_sem=send_b.at[hd, i],
            recv_sem=recv_b.at[hd, i],
            device_id={"dev": to},
            device_id_type=pl.DeviceIdType.MESH,
        )

    def copy_y(i):
        return pltpu.make_async_remote_copy(
            src_ref=ybuf.at[0],
            dst_ref=ybuf.at[i],
            send_sem=send_y.at[i],
            recv_sem=recv_y.at[i],
            device_id={"sub": lax.rem(sub + i, n_sub)},
            device_id_type=pl.DeviceIdType.MESH,
        )

    def owned(r):
        def look(n, found):
            first, second = found
            mine = dest_ref[n] == r
            return (
                jnp.where(mine, jnp.minimum(first, n), first),
                jnp.where(mine, jnp.maximum(second, n), second),
            )

        found = (jnp.int32(requests - 1), jnp.int32(0))
        if requests <= 8:
            for n in range(requests):
                found = look(n, found)
            return found
        return lax.fori_loop(0, requests, look, found)

    def decode_ahead(j, c):
        eight = iota((CHUNK, CHUNK), 0) == iota((CHUNK, CHUNK), 1)
        n = steps * CHUNK
        pieces = []
        total = jnp.zeros((1, CHUNK), F32)
        for s in range(steps):
            total = total + dd_ref[j, s : s + 1, c * CHUNK : (c + 1) * CHUNK]
            pieces.append(
                jnp.sum(
                    jnp.where(eight, jnp.broadcast_to(total, (CHUNK, CHUNK)), 0.0),
                    axis=1,
                    keepdims=True,
                )
            )
        col = jnp.concatenate(pieces, axis=0)
        square_row, square_col = iota((n, n), 0), iota((n, n), 1)
        row = jnp.sum(
            jnp.where(square_row == square_col, jnp.broadcast_to(col, (n, n)), 0.0),
            axis=0,
            keepdims=True,
        )
        seen = ((square_row & (CHUNK - 1)) == (square_col & (CHUNK - 1))) & (
            square_row >= square_col
        )
        weights = jnp.where(seen, jnp.exp(jnp.where(seen, col - row, 0.0)), 0.0)
        spread = (
            iota((rows, lanes), 0) == lax.rem(iota((rows, lanes), 1), rows)
        ).astype(BF16)
        own = iota((CHUNK, lanes), 0) == lax.div(iota((CHUNK, lanes), 1), rows)

        def diagonal_blocks(ref):
            return jnp.concatenate(
                [
                    jnp.where(
                        own,
                        dot(ref[j, s, :, c * CHUNK : (c + 1) * CHUNK], spread, TN),
                        0.0,
                    )
                    for s in range(steps)
                ],
                axis=0,
            )

        qb = diagonal_blocks(qd_ref).astype(BF16)
        kb = diagonal_blocks(kd_ref)
        vb = jnp.concatenate(
            [
                vd_ref[j, s, c * CHUNK : (c + 1) * CHUNK, :].astype(F32)
                for s in range(steps)
            ],
            axis=0,
        )
        mixed = dot(qb, kb.astype(BF16), NT) * weights
        ybuf[0, c, j] = dot(mixed, vb, NN, HIGHEST)
        tail = jnp.exp(jnp.concatenate([pieces[-1]] * steps, axis=0) - col)
        update = dot(kb * tail, vb, TN, HIGHEST)
        for h in range(CHUNK):
            fsbuf[j, c * CHUNK + h] = update[h * rows : (h + 1) * rows, :]
        qbuf[c, j] = qb
        ebuf[c, j] = jnp.broadcast_to(jnp.exp(col), (n, width))

    def decode(j, c):
        per = CHUNK // heads
        last = (steps - 1) * CHUNK
        parts = [
            rbuf[c * per + h // heads, h % heads, j] for h in range(CHUNK)
        ]
        high, low = split(jnp.concatenate(parts, axis=0))
        both = dot(qbuf[c, j], jnp.concatenate([high, low], axis=1), NN)
        ybuf[0, c, j] = (both[:, :width] + both[:, width:]) * ebuf[c, j] + ybuf[0, c, j]
        for h in range(CHUNK):
            fsbuf[j, c * CHUNK + h] = (
                parts[h] * ebuf[c, j, last + h : last + h + 1, :]
                + fsbuf[j, c * CHUNK + h]
            )

    for hd in range(heads):
        for g in range(group):
            dbuf[hd, g] = d_ref[hd, g : g + 1, :]
        each(0, group, functools.partial(state, hd))
        if hd == 0:
            pl.semaphore_wait(barrier, n_sub - 1 + n_dev - 1)
        each(1, n_sub, lambda i: copy_a(hd, i).start())
        mids[hd][pl.ds(sub * group, group)] = sbuf[hd, sub]

    for c in range(chunks):
        for j in range(slots):
            decode_ahead(j, c)

    def save(hd):
        return pltpu.make_async_copy(pbuf.at[hd], out_hbm.at[hd], local.at[hd])

    for hd in range(heads):
        each(1, n_sub, lambda i: copy_a(hd, i).wait_recv())

        def pass_on(i):
            first, second = owned(lax.rem(dev + i, n_dev))
            bbuf[hd, i, 0] = mids[hd][first]
            bbuf[hd, i, 1] = mids[hd][second]
            copy_b(hd, i).start()

        each(1, n_dev, pass_on)
        first, second = owned(dev)
        rbuf[dev, hd, 0] = mids[hd][first]
        rbuf[dev, hd, 1] = mids[hd][second]

    for hd in range(heads):
        each(0, group, functools.partial(output, hd))
        save(hd).start()

    for hd in range(heads):
        each(1, n_dev, lambda i: copy_b(hd, i).wait_recv())
    for c in range(chunks):
        for j in range(slots):
            decode(j, c)
    each(1, n_sub, lambda i: copy_y(i).start())
    final = pltpu.make_async_copy(fsbuf, fin_hbm, local.at[heads])
    final.start()
    share = all_heads // n_sub
    gates = [jax.nn.sigmoid(gate_ref[j].astype(F32)) * gain_ref[...] for j in range(slots)]
    each(1, n_sub, lambda i: copy_y(i).wait_recv())
    for j in range(slots):
        square = jnp.zeros((steps, width), F32)
        for c in range(chunks):
            y = ybuf[0, c, j]
            for i in range(1, n_sub):
                y = y + ybuf[i, c, j]
            for s in range(steps):
                ysum[j, s, c * CHUNK : (c + 1) * CHUNK, :] = y[
                    s * CHUNK : (s + 1) * CHUNK, :
                ]
            square = square + jnp.sum((y * y).reshape(steps, CHUNK, width), axis=1)
        mean = jnp.sum(square, axis=1, keepdims=True) / (all_heads * width)
        inverse = lax.rsqrt(mean + EPSILON)
        for h in range(share):
            y = jnp.concatenate(
                [ysum[j, s, pl.ds(sub * share + h, 1), :] for s in range(steps)], axis=0
            )
            gate = gates[j][:, h * width : (h + 1) * width]
            dec_ref[j, :, h * width : (h + 1) * width] = (y * inverse * gate).astype(
                BF16
            )
    for hd in range(heads):
        each(1, n_sub, lambda i: copy_a(hd, i).wait_send())
        each(1, n_dev, lambda i: copy_b(hd, i).wait_send())
        save(hd).wait()
    each(1, n_sub, lambda i: copy_y(i).wait_send())
    final.wait()


def body(n_dev, n_sub, *args):
    q, _, _, _, _, dest, qd = args[:7]
    heads, group, length, width = q.shape
    slots, steps, rows, all_heads = qd.shape
    requests = dest.shape[0]
    chunks = all_heads // CHUNK
    args = args[:11] + (args[11].reshape(1, -1),)
    vmem = pl.BlockSpec(memory_space=pltpu.VMEM)
    smem = pl.BlockSpec(memory_space=pltpu.SMEM)
    hbm = pl.BlockSpec(memory_space=pl.ANY)
    dma = pltpu.SemaphoreType.DMA
    return pl.pallas_call(
        functools.partial(kernel, n_dev, n_sub),
        out_shape=(
            jax.ShapeDtypeStruct(q.shape, BF16),
            jax.ShapeDtypeStruct(args[10].shape, BF16),
            jax.ShapeDtypeStruct((slots, all_heads, rows, width), F32),
        ),
        in_specs=[vmem] * 4 + [smem] * 2 + [vmem] * 6,
        out_specs=(hbm, vmem, hbm),
        scratch_shapes=[
            pltpu.VMEM((heads, n_sub, group, rows, width), F32),
            pltpu.VMEM((heads, n_dev, slots, rows, width), F32),
            pltpu.VMEM((n_dev, heads, slots, rows, width), F32),
            pltpu.VMEM((slots, all_heads, rows, width), F32),
            pltpu.VMEM(q.shape, BF16),
            pltpu.VMEM((heads, group, 1, length), F32),
            pltpu.VMEM((chunks, slots, steps * CHUNK, CHUNK * rows), BF16),
            pltpu.VMEM((chunks, slots, steps * CHUNK, width), F32),
            pltpu.VMEM((n_sub, chunks, slots, steps * CHUNK, width), F32),
            pltpu.VMEM((slots, steps, all_heads, width), F32),
            dma((heads, n_sub)),
            dma((heads, n_sub)),
            dma((heads, n_dev)),
            dma((heads, n_dev)),
            dma((n_sub,)),
            dma((n_sub,)),
            dma((heads + 1,)),
        ]
        + [pltpu.VMEM((requests, rows, width), F32)] * heads,
        compiler_params=pltpu.CompilerParams(
            collective_id=0, has_side_effects=True, vmem_limit_bytes=48 * 2**20
        ),
    )(*args)


def solution(mesh):
    placed = (
        P("dev", ("groups", "sub"), None, None),
        P("dev", ("groups", "sub"), None, None),
        P("dev", ("groups", "sub"), None, None),
        P("dev", ("groups", "sub"), None),
        P("groups"),
        P("groups"),
        P(("groups", "dev"), None, "sub", None),
        P(("groups", "dev"), None, "sub", None),
        P(("groups", "dev"), None, None, None),
        P(("groups", "dev"), None, None),
        P(("groups", "dev"), None, "sub"),
        P("sub"),
    )
    return jax.shard_map(
        functools.partial(body, mesh.shape["dev"], mesh.shape["sub"]),
        mesh=mesh,
        in_specs=placed,
        out_specs=(
            P("dev", ("groups", "sub"), None, None),
            P(("groups", "dev"), None, "sub"),
            P(("groups", "dev"), None, "sub", None),
        ),
        check_vma=False,
    )
```

time: 79.5 us -> 26.9 us (0.34)
  waiting for transfers between devices: 32 us -> 0 us
  Pallas kernels: 0 us -> 19.5 us
  between operations: 14.3 us -> 0.73 us
  starting transfers between devices: 7.53 us -> 0 us
  other arithmetic: 6.12 us -> 0 us
  blocking collectives: 5.73 us -> 0 us
  matrix products: 5.07 us -> 0 us
  local copies, waits for them, and re-layouts: 8.12 us -> 6.35 us
    unnamed x2 -> x0, waiting for transfers between devices: 21 us -> none
    pallas_call x0 -> x1, Pallas kernels: none -> 19.5 us  [body(): pl.pallas_call(functools.partial(kernel, n_dev, n_sub), out_shape=(jax.Sh...]
    all_to_all x1 -> x0, waiting for transfers between devices: 11 us -> none  [body(): lax.all_to_all(outgoing, ('dev', 'sub'), split_axis=0, concat_axis=0, til...]
    all_to_all x1 -> x0, starting transfers between devices: 7.49 us -> none  [body(): lax.all_to_all(outgoing, ('dev', 'sub'), split_axis=0, concat_axis=0, til...]
    psum x1 -> x0, blocking collectives: 5.73 us -> none  [body(): square_sum = lax.psum(jnp.sum(own_share * own_share, axis=-1), 'sub')]
    dot_general x14 -> x0, matrix products: 5.07 us -> none  [the longest x2 0.97 us: prefill_blocks(): jnp.einsum('hgtd,hgte->hgde', key_block.astype(jnp.float32) * tail_decay[...]
    another operation x2 -> x0, other arithmetic: 1.22 us -> none  [prefill_blocks(): jnp.cumsum(log_decay[:, :, block_start:block_start + BLOCK_POSITIONS], ax...]
    mul x4 -> x0, other arithmetic: 1.21 us -> none  [the longest x1 1.12 us: prefill_blocks(): key_input = key_input * valid_mask.astype(jnp.bfloat16)[None, :, :, None]]
  transfers between devices with their start and end apart: 2 -> 0, of which waited for: 2 -> 0; matrix products, arithmetic and copies ran while one was open for 4% -> 0% of each run, Pallas kernels for 0% -> 0%
where the time goes in v1:
time: 26.9 us; the launch traced here: 26.6 us
  Pallas kernels  19.5 us (72%)
  local copies, waits for them, and re-layouts  6.35 us (24%)
  between operations  0.73 us (3%)
    pallas_call x1, Pallas kernels, body(): pl.pallas_call(functools.partial(kernel, n_dev, n_sub), out_shape=(jax.Sh...  19.5 us
    unnamed x27, local copies, waits for them, and re-layouts  6.35 us

profile of v1, /device:TPU:0, one launch (start us, length us, event | category | flops | bytes accessed | tf_op | source)
XLA Modules:
  0.0 26.6 jit_solution(4797469459683716174)
XLA Ops:
  0.6 0.0 copy-start.10
  0.6 0.8 %copy.15.qd_ref = bf16[2,4,32,8]{3,2,1,0:T(8,128)(2,1)S(1)} copy(bf16[2,4,32,8]{2,3,1,0:T(8,128)(2,1)} %param.18) | data formatting | bytes 8192 | tf_op args[6]
  1.5 0.0 copy-done.10
  1.5 0.0 copy-start.3
  1.5 0.0 copy-start.4
  1.5 0.0 copy-start.5
  1.5 0.0 copy-start.6
  1.5 0.0 copy-start.7
  1.5 0.0 copy-start.8
  1.5 0.0 copy-start.9
  1.6 0.1 copy.16.kd_ref
  1.7 0.5 %copy-done.3 = bf16[2,4,8,128]{3,2,1,0:T(8,128)(2,1)S(1)} copy-done((bf16[2,4,8,128]{3,2,1,0:T(8,128)(2,1)S(1)}, bf16[2,4,8,128]{3,2,1,0:T(8,128)(2,1)}, u32[]{:S(2)}) %copy-start.3) | copy-done | bytes 16408
  2.2 0.0 copy-done.4
  2.2 0.0 copy-done.5
  2.2 0.0 copy-done.6
  2.2 0.0 copy-done.7
  2.2 0.0 copy-done.8
  2.2 0.0 copy-done.9
  2.2 0.0 copy-start
  2.2 0.9 %copy-done = bf16[2,2,256,128]{3,2,1,0:T(8,128)(2,1)S(1)} copy-done((bf16[2,2,256,128]{3,2,1,0:T(8,128)(2,1)S(1)}, bf16[2,2,256,128]{3,2,1,0:T(8,128)(2,1)}, u32[]{:S(2)}) %copy-start) | copy-done | bytes 262168
  3.2 0.0 copy-start.1
  3.2 0.9 %copy-done.1 = bf16[2,2,256,128]{3,2,1,0:T(8,128)(2,1)S(1)} copy-done((bf16[2,2,256,128]{3,2,1,0:T(8,128)(2,1)S(1)}, bf16[2,2,256,128]{3,2,1,0:T(8,128)(2,1)}, u32[]{:S(2)}) %copy-start.1) | copy-done | bytes 262168
  4.1 0.0 copy-start.2
  4.1 0.9 %copy-done.2 = bf16[2,2,256,128]{3,2,1,0:T(8,128)(2,1)S(1)} copy-done((bf16[2,2,256,128]{3,2,1,0:T(8,128)(2,1)S(1)}, bf16[2,2,256,128]{3,2,1,0:T(8,128)(2,1)}, u32[]{:S(2)}) %copy-start.2) | copy-done | bytes 262168
  5.1 19.5 %shard_map.139 = (bf16[2,2,256,128]{3,2,1,0:T(8,128)(2,1)S(1)}, bf16[2,4,256]{2,1,0:T(4,128)(2,1)S(1)}, f32[2,8,32,128]{3,2,1,0:T(8,128)S(1)}) custom-call(bf16[2,2,256,128]{3,2,1,0:T(8,128)(2,1)S(1)} %copy-done, bf16[2,2,256,128]{3,2,1,0:T(8,128)(2,1)S(1)} %copy-done.1, bf16[2,2,256,128]{3,2,1,0:T(8,128)(2,1)S(1)} %copy-done.2, f32[2,2,256]{2,1,0:T(2,128)S(1)} %copy-done.4, ...), custom_call_target="tpu_custom_call" | custom-call | tf_op jit(solution)/shard_map/pallas_call | solution.py:396
  24.6 0.7 %copy.20 = bf16[2,2,256,128]{3,2,1,0:T(8,128)(2,1)} copy(bf16[2,2,256,128]{3,2,1,0:T(8,128)(2,1)S(1)} %get-tuple-element.6) | data formatting | bytes 524288
  25.3 0.6 %copy.21 = bf16[2,4,256]{2,1,0:T(4,128)(2,1)} copy(bf16[2,4,256]{2,1,0:T(4,128)(2,1)S(1)} %get-tuple-element.7) | data formatting | bytes 8192
  25.9 0.7 %copy.22 = f32[2,8,32,128]{3,2,1,0:T(8,128)} copy(f32[2,8,32,128]{3,2,1,0:T(8,128)S(1)} %get-tuple-element.8) | data formatting | bytes 524288
Async XLA Ops:
  0.6 0.8 %copy-start.10 = (bf16[2,4,32,8]{2,3,1,0:T(8,128)(2,1)S(1)}, bf16[2,4,32,8]{2,3,1,0:T(8,128)(2,1)}, u32[]{:S(2)}) copy-start(bf16[2,4,32,8]{2,3,1,0:T(8,128)(2,1)} %param.19) | copy-start | bytes 12292
  1.5 0.7 %copy-start.3 = (bf16[2,4,8,128]{3,2,1,0:T(8,128)(2,1)S(1)}, bf16[2,4,8,128]{3,2,1,0:T(8,128)(2,1)}, u32[]{:S(2)}) copy-start(bf16[2,4,8,128]{3,2,1,0:T(8,128)(2,1)} %vd_ref.1) | copy-start | bytes 49156
  1.5 0.7 %copy-start.4 = (f32[2,2,256]{2,1,0:T(2,128)S(1)}, f32[2,2,256]{2,1,0:T(2,128)}, u32[]{:S(2)}) copy-start(f32[2,2,256]{2,1,0:T(2,128)} %d_ref.1) | copy-start | bytes 12292
  1.5 0.7 %copy-start.5 = (f32[2,4,8]{2,1,0:T(4,128)S(1)}, f32[2,4,8]{2,1,0:T(4,128)}, u32[]{:S(2)}) copy-start(f32[2,4,8]{2,1,0:T(4,128)} %dd_ref.1) | copy-start | bytes 772
  1.5 0.7 %copy-start.6 = (bf16[2,4,256]{2,1,0:T(4,128)(2,1)S(1)}, bf16[2,4,256]{2,1,0:T(4,128)(2,1)}, u32[]{:S(2)}) copy-start(bf16[2,4,256]{2,1,0:T(4,128)(2,1)} %gate_ref.1) | copy-start | bytes 12292
  1.5 0.7 %copy-start.7 = (f32[256]{0:T(256)S(1)}, f32[256]{0:T(256)}, u32[]{:S(2)}) copy-start(f32[256]{0:T(256)} %param.23) | copy-start | bytes 3076
  1.5 0.7 %copy-start.8 = (s32[8]{0:T(128)S(1)}, s32[8]{0:T(128)}, u32[]{:S(2)}) copy-start(s32[8]{0:T(128)} %blocks_ref.1) | copy-start | bytes 100
  1.5 0.7 %copy-start.9 = (s32[8]{0:T(128)S(1)}, s32[8]{0:T(128)}, u32[]{:S(2)}) copy-start(s32[8]{0:T(128)} %dest_ref.1) | copy-start | bytes 100
  2.2 1.0 %copy-start = (bf16[2,2,256,128]{3,2,1,0:T(8,128)(2,1)S(1)}, bf16[2,2,256,128]{3,2,1,0:T(8,128)(2,1)}, u32[]{:S(2)}) copy-start(bf16[2,2,256,128]{3,2,1,0:T(8,128)(2,1)} %q_ref.1) | copy-start | bytes 786436
  3.2 0.9 %copy-start.1 = (bf16[2,2,256,128]{3,2,1,0:T(8,128)(2,1)S(1)}, bf16[2,2,256,128]{3,2,1,0:T(8,128)(2,1)}, u32[]{:S(2)}) copy-start(bf16[2,2,256,128]{3,2,1,0:T(8,128)(2,1)} %k_ref.1) | copy-start | bytes 786436
  4.1 0.9 %copy-start.2 = (bf16[2,2,256,128]{3,2,1,0:T(8,128)(2,1)S(1)}, bf16[2,2,256,128]{3,2,1,0:T(8,128)(2,1)}, u32[]{:S(2)}) copy-start(bf16[2,2,256,128]{3,2,1,0:T(8,128)(2,1)} %v_ref.1) | copy-start | bytes 786436

commit v2 on v1

--- a/solution.py
+++ b/solution.py
@@ -51,31 +51,33 @@
 def kernel(
     n_dev,
     n_sub,
+    q_hbm,
+    k_hbm,
+    v_hbm,
+    d_hbm,
+    blocks_ref,
+    dest_ref,
+    qd_hbm,
+    kd_hbm,
+    vd_hbm,
+    dd_hbm,
+    pbuf,
+    fsbuf,
+    ybuf,
     q_ref,
     k_ref,
     v_ref,
     d_ref,
-    blocks_ref,
-    dest_ref,
     qd_ref,
     kd_ref,
     vd_ref,
     dd_ref,
-    gate_ref,
-    gain_ref,
-    out_hbm,
-    dec_ref,
-    fin_hbm,
     sbuf,
     bbuf,
     rbuf,
-    fsbuf,
-    pbuf,
     dbuf,
     qbuf,
     ebuf,
-    ybuf,
-    ysum,
     send_a,
     recv_a,
     send_b,
@@ -87,13 +89,30 @@
 ):
     heads, group, length, width = q_ref.shape
     prompt_blocks = length // BLOCK
-    slots, steps, rows, all_heads = qd_ref.shape
+    slots, steps, all_heads, rows = qd_ref.shape
     requests = dest_ref.shape[0]
     chunks = all_heads // CHUNK
     lanes = CHUNK * rows
     sub = lax.axis_index("sub")
     dev = lax.axis_index("dev")
 
+    loads = [
+        pltpu.make_async_copy(source, target, local.at[i])
+        for i, (source, target) in enumerate(
+            (
+                (d_hbm, d_ref),
+                (v_hbm, v_ref),
+                (k_hbm, k_ref),
+                (q_hbm, q_ref),
+                (dd_hbm, dd_ref),
+                (kd_hbm, kd_ref),
+                (qd_hbm, qd_ref),
+                (vd_hbm, vd_ref),
+            )
+        )
+    ]
+    for load in loads:
+        load.start()
     barrier = pltpu.get_barrier_semaphore()
 
     def greet_sub(i):
@@ -267,7 +286,7 @@
                 [
                     jnp.where(
                         own,
-                        dot(ref[j, s, :, c * CHUNK : (c + 1) * CHUNK], spread, TN),
+                        dot(ref[j, s, c * CHUNK : (c + 1) * CHUNK, :], spread, NN),
                         0.0,
                     )
                     for s in range(steps)
@@ -308,6 +327,8 @@
                 + fsbuf[j, c * CHUNK + h]
             )
 
+    for load in loads[:3]:
+        load.wait()
     for hd in range(heads):
         for g in range(group):
             dbuf[hd, g] = d_ref[hd, g : g + 1, :]
@@ -316,13 +337,8 @@
             pl.semaphore_wait(barrier, n_sub - 1 + n_dev - 1)
         each(1, n_sub, lambda i: copy_a(hd, i).start())
         mids[hd][pl.ds(sub * group, group)] = sbuf[hd, sub]
-
-    for c in range(chunks):
-        for j in range(slots):
-            decode_ahead(j, c)
-
-    def save(hd):
-        return pltpu.make_async_copy(pbuf.at[hd], out_hbm.at[hd], local.at[hd])
+    for load in loads[3:]:
+        load.wait()
 
     for hd in range(heads):
         each(1, n_sub, lambda i: copy_a(hd, i).wait_recv())
@@ -337,10 +353,13 @@
         first, second = owned(dev)
         rbuf[dev, hd, 0] = mids[hd][first]
         rbuf[dev, hd, 1] = mids[hd][second]
-
-    for hd in range(heads):
-        each(0, group, functools.partial(output, hd))
-        save(hd).start()
+        if hd + 1 < heads:
+            each(0, group, functools.partial(output, hd))
+
+    for c in range(chunks):
+        for j in range(slots):
+            decode_ahead(j, c)
+    each(0, group, functools.partial(output, heads - 1))
 
     for hd in range(heads):
         each(1, n_dev, lambda i: copy_b(hd, i).wait_recv())
@@ -348,17 +367,31 @@
         for j in range(slots):
             decode(j, c)
     each(1, n_sub, lambda i: copy_y(i).start())
-    final = pltpu.make_async_copy(fsbuf, fin_hbm, local.at[heads])
-    final.start()
+    for hd in range(heads):
+        each(1, n_sub, lambda i: copy_a(hd, i).wait_send())
+        each(1, n_dev, lambda i: copy_b(hd, i).wait_send())
+    each(1, n_sub, lambda i: copy_y(i).wait())
+
+
+def finish(
+    n_sub, out_ref, fin_ref, y_ref, gate_ref, gain_ref, out_hbm, dec_ref, fin_hbm, ysum, sems
+):
+    saves = [
+        pltpu.make_async_copy(out_ref, out_hbm, sems.at[0]),
+        pltpu.make_async_copy(fin_ref, fin_hbm, sems.at[1]),
+    ]
+    for save in saves:
+        save.start()
+    _, chunks, slots, _, width = y_ref.shape
+    _, steps, all_heads, _ = ysum.shape
+    sub = lax.axis_index("sub")
     share = all_heads // n_sub
-    gates = [jax.nn.sigmoid(gate_ref[j].astype(F32)) * gain_ref[...] for j in range(slots)]
-    each(1, n_sub, lambda i: copy_y(i).wait_recv())
     for j in range(slots):
         square = jnp.zeros((steps, width), F32)
         for c in range(chunks):
-            y = ybuf[0, c, j]
+            y = y_ref[0, c, j]
             for i in range(1, n_sub):
-                y = y + ybuf[i, c, j]
+                y = y + y_ref[i, c, j]
             for s in range(steps):
                 ysum[j, s, c * CHUNK : (c + 1) * CHUNK, :] = y[
                     s * CHUNK : (s + 1) * CHUNK, :
@@ -366,66 +399,94 @@
             square = square + jnp.sum((y * y).reshape(steps, CHUNK, width), axis=1)
         mean = jnp.sum(square, axis=1, keepdims=True) / (all_heads * width)
         inverse = lax.rsqrt(mean + EPSILON)
+        gates = jax.nn.sigmoid(gate_ref[j].astype(F32)) * gain_ref[...]
         for h in range(share):
             y = jnp.concatenate(
                 [ysum[j, s, pl.ds(sub * share + h, 1), :] for s in range(steps)], axis=0
             )
-            gate = gates[j][:, h * width : (h + 1) * width]
+            gate = gates[:, h * width : (h + 1) * width]
             dec_ref[j, :, h * width : (h + 1) * width] = (y * inverse * gate).astype(
                 BF16
             )
-    for hd in range(heads):
-        each(1, n_sub, lambda i: copy_a(hd, i).wait_send())
-        each(1, n_dev, lambda i: copy_b(hd, i).wait_send())
-        save(hd).wait()
-    each(1, n_sub, lambda i: copy_y(i).wait_send())
-    final.wait()
+    for save in saves:
+        save.wait()
 
 
 def body(n_dev, n_sub, *args):
-    q, _, _, _, _, dest, qd = args[:7]
+    q, k, v, d, blocks, dest, qd, kd, vd, dd, gate, gain = args
     heads, group, length, width = q.shape
     slots, steps, rows, all_heads = qd.shape
     requests = dest.shape[0]
     chunks = all_heads // CHUNK
-    args = args[:11] + (args[11].reshape(1, -1),)
     vmem = pl.BlockSpec(memory_space=pltpu.VMEM)
     smem = pl.BlockSpec(memory_space=pltpu.SMEM)
-    hbm = pl.BlockSpec(memory_space=pl.ANY)
+    hbm = pl.BlockSpec(memory_space=pltpu.HBM)
     dma = pltpu.SemaphoreType.DMA
-    return pl.pallas_call(
+    turned = (slots, steps, all_heads, rows)
+    state = jax.ShapeDtypeStruct((slots, all_heads, rows, width), F32)
+    parts = (n_sub, chunks, slots, steps * CHUNK, width)
+    made = pl.pallas_call(
         functools.partial(kernel, n_dev, n_sub),
         out_shape=(
             jax.ShapeDtypeStruct(q.shape, BF16),
-            jax.ShapeDtypeStruct(args[10].shape, BF16),
-            jax.ShapeDtypeStruct((slots, all_heads, rows, width), F32),
+            state,
+            jax.ShapeDtypeStruct(parts, F32),
         ),
-        in_specs=[vmem] * 4 + [smem] * 2 + [vmem] * 6,
-        out_specs=(hbm, vmem, hbm),
+        in_specs=[hbm] * 4 + [smem] * 2 + [hbm] * 4,
+        out_specs=(vmem, vmem, vmem),
         scratch_shapes=[
+            pltpu.VMEM(q.shape, BF16),
+            pltpu.VMEM(q.shape, BF16),
+            pltpu.VMEM(q.shape, BF16),
+            pltpu.VMEM(d.shape, F32),
+            pltpu.VMEM(turned, BF16),
+            pltpu.VMEM(turned, BF16),
+            pltpu.VMEM(vd.shape, BF16),
+            pltpu.VMEM(dd.shape, F32),
             pltpu.VMEM((heads, n_sub, group, rows, width), F32),
             pltpu.VMEM((heads, n_dev, slots, rows, width), F32),
             pltpu.VMEM((n_dev, heads, slots, rows, width), F32),
-            pltpu.VMEM((slots, all_heads, rows, width), F32),
-            pltpu.VMEM(q.shape, BF16),
             pltpu.VMEM((heads, group, 1, length), F32),
             pltpu.VMEM((chunks, slots, steps * CHUNK, CHUNK * rows), BF16),
             pltpu.VMEM((chunks, slots, steps * CHUNK, width), F32),
-            pltpu.VMEM((n_sub, chunks, slots, steps * CHUNK, width), F32),
-            pltpu.VMEM((slots, steps, all_heads, width), F32),
             dma((heads, n_sub)),
             dma((heads, n_sub)),
             dma((heads, n_dev)),
             dma((heads, n_dev)),
             dma((n_sub,)),
             dma((n_sub,)),
-            dma((heads + 1,)),
+            dma((8,)),
         ]
         + [pltpu.VMEM((requests, rows, width), F32)] * heads,
         compiler_params=pltpu.CompilerParams(
-            collective_id=0, has_side_effects=True, vmem_limit_bytes=48 * 2**20
+            collective_id=0, has_side_effects=True, vmem_limit_bytes=40 * 2**20
         ),
-    )(*args)
+    )(
+        q,
+        k,
+        v,
+        d,
+        blocks,
+        dest,
+        jnp.swapaxes(qd, 2, 3),
+        jnp.swapaxes(kd, 2, 3),
+        vd,
+        dd,
+    )
+    out, fin, y = made
+    out, dec, fin = pl.pallas_call(
+        functools.partial(finish, n_sub),
+        out_shape=(
+            jax.ShapeDtypeStruct(q.shape, BF16),
+            jax.ShapeDtypeStruct(gate.shape, BF16),
+            state,
+        ),
+        in_specs=[pl.BlockSpec(memory_space=pl.ANY)] * 2 + [vmem] * 3,
+        out_specs=(hbm, vmem, hbm),
+        scratch_shapes=[pltpu.VMEM((slots, steps, all_heads, width), F32), dma((2,))],
+        compiler_params=pltpu.CompilerParams(vmem_limit_bytes=16 * 2**20),
+    )(out, fin, y, gate, gain.reshape(1, -1))
+    return out, dec, fin
 
 
 def solution(mesh):

time: 26.9 us -> 29.2 us (1.086)
  Pallas kernels: 19.5 us -> 20.9 us
  local copies, waits for them, and re-layouts: 6.35 us -> 7.04 us
    pallas_call x0 -> x1, Pallas kernels: none -> 1.4 us  [body(): pl.pallas_call(functools.partial(finish, n_sub), out_shape=(jax.ShapeDtyp...]
    unnamed x27 -> x24, local copies, waits for them, and re-layouts: 6.35 us -> 7.04 us
where the time goes in v2:
time: 29.2 us; the launch traced here: 28.7 us
  Pallas kernels  20.9 us (72%)
  local copies, waits for them, and re-layouts  7.04 us (24%)
  between operations  0.69 us (2%)
    pallas_call x1, Pallas kernels, body(): pl.pallas_call(functools.partial(kernel, n_dev, n_sub), out_shape=(jax.Sh...  19.5 us
    unnamed x24, local copies, waits for them, and re-layouts  7.04 us
    pallas_call x1, Pallas kernels, body(): pl.pallas_call(functools.partial(finish, n_sub), out_shape=(jax.ShapeDtyp...  1.4 us

profile of v2, /device:TPU:0, one launch (start us, length us, event | category | flops | bytes accessed | tf_op | source)
XLA Modules:
  0.0 28.7 jit_solution(3329834271284412614)
XLA Ops:
  0.6 0.0 copy-start.6
  0.6 0.0 copy-start.10
  0.7 0.0 copy-start.11
  0.7 0.7 %copy-done.6 = f32[2,2,256]{2,1,0:T(2,128)S(1)} copy-done((f32[2,2,256]{2,1,0:T(2,128)S(1)}, f32[2,2,256]{2,1,0:T(2,128)}, u32[]{:S(2)}) %copy-start.6) | copy-done | bytes 4120
  1.3 0.0 copy-done.10
  1.3 0.0 copy-done.11
  1.3 0.0 copy-start
  1.3 0.9 %copy-done = bf16[2,2,256,128]{3,2,1,0:T(8,128)(2,1)S(1)} copy-done((bf16[2,2,256,128]{3,2,1,0:T(8,128)(2,1)S(1)}, bf16[2,2,256,128]{3,2,1,0:T(8,128)(2,1)}, u32[]{:S(2)}) %copy-start) | copy-done | bytes 262168
  2.3 0.0 copy-start.1
  2.3 0.9 %copy-done.1 = bf16[2,2,256,128]{3,2,1,0:T(8,128)(2,1)S(1)} copy-done((bf16[2,2,256,128]{3,2,1,0:T(8,128)(2,1)S(1)}, bf16[2,2,256,128]{3,2,1,0:T(8,128)(2,1)}, u32[]{:S(2)}) %copy-start.1) | copy-done | bytes 262168
  3.2 0.0 copy-start.2
  3.2 0.9 %copy-done.2 = bf16[2,2,256,128]{3,2,1,0:T(8,128)(2,1)S(1)} copy-done((bf16[2,2,256,128]{3,2,1,0:T(8,128)(2,1)S(1)}, bf16[2,2,256,128]{3,2,1,0:T(8,128)(2,1)}, u32[]{:S(2)}) %copy-start.2) | copy-done | bytes 262168
  4.2 0.0 copy-start.3
  4.2 0.7 %copy-done.3 = bf16[2,4,32,8]{2,3,1,0:T(8,128)(2,1)S(1)} copy-done((bf16[2,4,32,8]{2,3,1,0:T(8,128)(2,1)S(1)}, bf16[2,4,32,8]{2,3,1,0:T(8,128)(2,1)}, u32[]{:S(2)}) %copy-start.3) | copy-done | bytes 4120
  4.9 0.0 copy-start.4
  4.9 0.7 %copy-done.4 = bf16[2,4,32,8]{2,3,1,0:T(8,128)(2,1)S(1)} copy-done((bf16[2,4,32,8]{2,3,1,0:T(8,128)(2,1)S(1)}, bf16[2,4,32,8]{2,3,1,0:T(8,128)(2,1)}, u32[]{:S(2)}) %copy-start.4) | copy-done | bytes 4120
  5.6 0.0 copy-start.5
  5.6 0.7 %copy-done.5 = bf16[2,4,8,128]{3,2,1,0:T(8,128)(2,1)S(1)} copy-done((bf16[2,4,8,128]{3,2,1,0:T(8,128)(2,1)S(1)}, bf16[2,4,8,128]{3,2,1,0:T(8,128)(2,1)}, u32[]{:S(2)}) %copy-start.5) | copy-done | bytes 16408
  6.3 0.0 copy-start.7
  6.3 0.7 %copy-done.7 = f32[2,4,8]{2,1,0:T(4,128)S(1)} copy-done((f32[2,4,8]{2,1,0:T(4,128)S(1)}, f32[2,4,8]{2,1,0:T(4,128)}, u32[]{:S(2)}) %copy-start.7) | copy-done | bytes 280
  7.0 19.5 %shard_map.139 = (bf16[2,2,256,128]{3,2,1,0:T(8,128)(2,1)S(1)}, f32[2,8,32,128]{3,2,1,0:T(8,128)S(1)}, f32[4,1,2,32,128]{4,3,2,1,0:T(8,128)S(1)}) custom-call(bf16[2,2,256,128]{3,2,1,0:T(8,128)(2,1)S(1)} %copy-done, bf16[2,2,256,128]{3,2,1,0:T(8,128)(2,1)S(1)} %copy-done.1, bf16[2,2,256,128]{3,2,1,0:T(8,128)(2,1)S(1)} %copy-done.2, ...), custom_call_target="tpu_custom_call" | custom-call | tf_op jit(solution)/shard_map/pallas_call | solution.py:428
  26.6 0.0 copy-start.8
  26.6 0.0 copy-start.9
  26.6 0.7 %copy-done.8 = bf16[2,4,256]{2,1,0:T(4,128)(2,1)S(1)} copy-done((bf16[2,4,256]{2,1,0:T(4,128)(2,1)S(1)}, bf16[2,4,256]{2,1,0:T(4,128)(2,1)}, u32[]{:S(2)}) %copy-start.8) | copy-done | bytes 4120
  27.2 0.0 copy-done.9
  27.3 1.4 %shard_map.140 = (bf16[2,2,256,128]{3,2,1,0:T(8,128)(2,1)}, bf16[2,4,256]{2,1,0:T(4,128)(2,1)}, f32[2,8,32,128]{3,2,1,0:T(8,128)}) custom-call(bf16[2,2,256,128]{3,2,1,0:T(8,128)(2,1)S(1)} %get-tuple-element.6.out_ref, f32[2,8,32,128]{3,2,1,0:T(8,128)S(1)} %get-tuple-element.7.fin_ref, f32[4,1,2,32,128]{4,3,2,1,0:T(8,128)S(1)} %get-tuple-element.8.y_ref, ...), custom_call_target="tpu_custom_call" | custom-call | tf_op jit(solution)/shard_map/pallas_call | solution.py:477
Async XLA Ops:
  0.6 0.7 %copy-start.6 = (f32[2,2,256]{2,1,0:T(2,128)S(1)}, f32[2,2,256]{2,1,0:T(2,128)}, u32[]{:S(2)}) copy-start(f32[2,2,256]{2,1,0:T(2,128)} %d_hbm.1) | copy-start | bytes 12292
  0.6 0.7 %copy-start.10 = (s32[8]{0:T(128)S(1)}, s32[8]{0:T(128)}, u32[]{:S(2)}) copy-start(s32[8]{0:T(128)} %blocks_ref.1) | copy-start | bytes 100
  0.7 0.7 %copy-start.11 = (s32[8]{0:T(128)S(1)}, s32[8]{0:T(128)}, u32[]{:S(2)}) copy-start(s32[8]{0:T(128)} %dest_ref.1) | copy-start | bytes 100
  1.3 1.0 %copy-start = (bf16[2,2,256,128]{3,2,1,0:T(8,128)(2,1)S(1)}, bf16[2,2,256,128]{3,2,1,0:T(8,128)(2,1)}, u32[]{:S(2)}) copy-start(bf16[2,2,256,128]{3,2,1,0:T(8,128)(2,1)} %q_hbm.1) | copy-start | bytes 786436
  2.3 0.9 %copy-start.1 = (bf16[2,2,256,128]{3,2,1,0:T(8,128)(2,1)S(1)}, bf16[2,2,256,128]{3,2,1,0:T(8,128)(2,1)}, u32[]{:S(2)}) copy-start(bf16[2,2,256,128]{3,2,1,0:T(8,128)(2,1)} %k_hbm.1) | copy-start | bytes 786436
  3.2 0.9 %copy-start.2 = (bf16[2,2,256,128]{3,2,1,0:T(8,128)(2,1)S(1)}, bf16[2,2,256,128]{3,2,1,0:T(8,128)(2,1)}, u32[]{:S(2)}) copy-start(bf16[2,2,256,128]{3,2,1,0:T(8,128)(2,1)} %v_hbm.1) | copy-start | bytes 786436
  4.2 0.7 %copy-start.3 = (bf16[2,4,32,8]{2,3,1,0:T(8,128)(2,1)S(1)}, bf16[2,4,32,8]{2,3,1,0:T(8,128)(2,1)}, u32[]{:S(2)}) copy-start(bf16[2,4,32,8]{2,3,1,0:T(8,128)(2,1)} %param.18) | copy-start | bytes 12292
  4.9 0.7 %copy-start.4 = (bf16[2,4,32,8]{2,3,1,0:T(8,128)(2,1)S(1)}, bf16[2,4,32,8]{2,3,1,0:T(8,128)(2,1)}, u32[]{:S(2)}) copy-start(bf16[2,4,32,8]{2,3,1,0:T(8,128)(2,1)} %param.19) | copy-start | bytes 12292
  5.6 0.7 %copy-start.5 = (bf16[2,4,8,128]{3,2,1,0:T(8,128)(2,1)S(1)}, bf16[2,4,8,128]{3,2,1,0:T(8,128)(2,1)}, u32[]{:S(2)}) copy-start(bf16[2,4,8,128]{3,2,1,0:T(8,128)(2,1)} %vd_hbm.1) | copy-start | bytes 49156
  6.3 0.7 %copy-start.7 = (f32[2,4,8]{2,1,0:T(4,128)S(1)}, f32[2,4,8]{2,1,0:T(4,128)}, u32[]{:S(2)}) copy-start(f32[2,4,8]{2,1,0:T(4,128)} %dd_hbm.1) | copy-start | bytes 772
  26.6 0.7 %copy-start.8 = (bf16[2,4,256]{2,1,0:T(4,128)(2,1)S(1)}, bf16[2,4,256]{2,1,0:T(4,128)(2,1)}, u32[]{:S(2)}) copy-start(bf16[2,4,256]{2,1,0:T(4,128)(2,1)} %gate_ref.1) | copy-start | bytes 12292
  26.6 0.7 %copy-start.9 = (f32[256]{0:T(256)S(1)}, f32[256]{0:T(256)}, u32[]{:S(2)}) copy-start(f32[256]{0:T(256)} %param.23) | copy-start | bytes 3076

commit v3 on v2

--- a/solution.py
+++ b/solution.py
@@ -61,9 +61,17 @@
     kd_hbm,
     vd_hbm,
     dd_hbm,
+    gate_hbm,
+    gain_hbm,
+    out_hbm,
+    dec_ref,
+    fin_hbm,
     pbuf,
     fsbuf,
     ybuf,
+    ysum,
+    gate_ref,
+    gain_ref,
     q_ref,
     k_ref,
     v_ref,
@@ -85,6 +93,7 @@
     send_y,
     recv_y,
     local,
+    saved,
     *mids,
 ):
     heads, group, length, width = q_ref.shape
@@ -108,6 +117,8 @@
                 (kd_hbm, kd_ref),
                 (qd_hbm, qd_ref),
                 (vd_hbm, vd_ref),
+                (gate_hbm, gate_ref),
+                (gain_hbm, gain_ref),
             )
         )
     ]
@@ -340,6 +351,9 @@
     for load in loads[3:]:
         load.wait()
 
+    def save(hd):
+        return pltpu.make_async_copy(pbuf.at[hd], out_hbm.at[hd], saved.at[hd])
+
     for hd in range(heads):
         each(1, n_sub, lambda i: copy_a(hd, i).wait_recv())
 
@@ -355,11 +369,13 @@
         rbuf[dev, hd, 1] = mids[hd][second]
         if hd + 1 < heads:
             each(0, group, functools.partial(output, hd))
+            save(hd).start()
 
     for c in range(chunks):
         for j in range(slots):
             decode_ahead(j, c)
     each(0, group, functools.partial(output, heads - 1))
+    save(heads - 1).start()
 
     for hd in range(heads):
         each(1, n_dev, lambda i: copy_b(hd, i).wait_recv())
@@ -367,31 +383,23 @@
         for j in range(slots):
             decode(j, c)
     each(1, n_sub, lambda i: copy_y(i).start())
+    final = pltpu.make_async_copy(fsbuf, fin_hbm, saved.at[heads])
+    final.start()
+    share = all_heads // n_sub
+    gates = [
+        jax.nn.sigmoid(gate_ref[j].astype(F32)) * gain_ref[...] for j in range(slots)
+    ]
     for hd in range(heads):
         each(1, n_sub, lambda i: copy_a(hd, i).wait_send())
         each(1, n_dev, lambda i: copy_b(hd, i).wait_send())
-    each(1, n_sub, lambda i: copy_y(i).wait())
-
-
-def finish(
-    n_sub, out_ref, fin_ref, y_ref, gate_ref, gain_ref, out_hbm, dec_ref, fin_hbm, ysum, sems
-):
-    saves = [
-        pltpu.make_async_copy(out_ref, out_hbm, sems.at[0]),
-        pltpu.make_async_copy(fin_ref, fin_hbm, sems.at[1]),
-    ]
-    for save in saves:
-        save.start()
-    _, chunks, slots, _, width = y_ref.shape
-    _, steps, all_heads, _ = ysum.shape
-    sub = lax.axis_index("sub")
-    share = all_heads // n_sub
+        save(hd).wait()
+    each(1, n_sub, lambda i: copy_y(i).wait_recv())
     for j in range(slots):
         square = jnp.zeros((steps, width), F32)
         for c in range(chunks):
-            y = y_ref[0, c, j]
+            y = ybuf[0, c, j]
             for i in range(1, n_sub):
-                y = y + y_ref[i, c, j]
+                y = y + ybuf[i, c, j]
             for s in range(steps):
                 ysum[j, s, c * CHUNK : (c + 1) * CHUNK, :] = y[
                     s * CHUNK : (s + 1) * CHUNK, :
@@ -399,15 +407,26 @@
             square = square + jnp.sum((y * y).reshape(steps, CHUNK, width), axis=1)
         mean = jnp.sum(square, axis=1, keepdims=True) / (all_heads * width)
         inverse = lax.rsqrt(mean + EPSILON)
-        gates = jax.nn.sigmoid(gate_ref[j].astype(F32)) * gain_ref[...]
         for h in range(share):
             y = jnp.concatenate(
                 [ysum[j, s, pl.ds(sub * share + h, 1), :] for s in range(steps)], axis=0
             )
-            gate = gates[:, h * width : (h + 1) * width]
+            gate = gates[j][:, h * width : (h + 1) * width]
             dec_ref[j, :, h * width : (h + 1) * width] = (y * inverse * gate).astype(
                 BF16
             )
+    each(1, n_sub, lambda i: copy_y(i).wait_send())
+    final.wait()
+
+
+def finish(*refs):
+    sems = refs[-1]
+    half = (len(refs) - 1) // 2
+    saves = [
+        pltpu.make_async_copy(refs[i], refs[half + i], sems.at[i]) for i in range(half)
+    ]
+    for save in saves:
+        save.start()
     for save in saves:
         save.wait()
 
@@ -424,17 +443,23 @@
     dma = pltpu.SemaphoreType.DMA
     turned = (slots, steps, all_heads, rows)
     state = jax.ShapeDtypeStruct((slots, all_heads, rows, width), F32)
-    parts = (n_sub, chunks, slots, steps * CHUNK, width)
+    shapes = (
+        jax.ShapeDtypeStruct(q.shape, BF16),
+        jax.ShapeDtypeStruct(gate.shape, BF16),
+        state,
+    )
     made = pl.pallas_call(
         functools.partial(kernel, n_dev, n_sub),
-        out_shape=(
-            jax.ShapeDtypeStruct(q.shape, BF16),
-            state,
-            jax.ShapeDtypeStruct(parts, F32),
-        ),
-        in_specs=[hbm] * 4 + [smem] * 2 + [hbm] * 4,
-        out_specs=(vmem, vmem, vmem),
+        out_shape=shapes,
+        in_specs=[hbm] * 4 + [smem] * 2 + [hbm] * 6,
+        out_specs=(hbm, vmem, hbm),
         scratch_shapes=[
+            pltpu.VMEM(q.shape, BF16),
+            pltpu.VMEM(state.shape, F32),
+            pltpu.VMEM((n_sub, chunks, slots, steps * CHUNK, width), F32),
+            pltpu.VMEM((slots, steps, all_heads, width), F32),
+            pltpu.VMEM(gate.shape, BF16),
+            pltpu.VMEM((1, gain.shape[0]), F32),
             pltpu.VMEM(q.shape, BF16),
             pltpu.VMEM(q.shape, BF16),
             pltpu.VMEM(q.shape, BF16),
@@ -455,11 +480,12 @@
             dma((heads, n_dev)),
             dma((n_sub,)),
             dma((n_sub,)),
-            dma((8,)),
+            dma((10,)),
+            dma((heads + 1,)),
         ]
         + [pltpu.VMEM((requests, rows, width), F32)] * heads,
         compiler_params=pltpu.CompilerParams(
-            collective_id=0, has_side_effects=True, vmem_limit_bytes=40 * 2**20
+            collective_id=0, has_side_effects=True, vmem_limit_bytes=64 * 2**20
         ),
     )(
         q,
@@ -472,21 +498,17 @@
         jnp.swapaxes(kd, 2, 3),
         vd,
         dd,
+        gate,
+        gain.reshape(1, -1),
     )
-    out, fin, y = made
-    out, dec, fin = pl.pallas_call(
-        functools.partial(finish, n_sub),
-        out_shape=(
-            jax.ShapeDtypeStruct(q.shape, BF16),
-            jax.ShapeDtypeStruct(gate.shape, BF16),
-            state,
-        ),
-        in_specs=[pl.BlockSpec(memory_space=pl.ANY)] * 2 + [vmem] * 3,
-        out_specs=(hbm, vmem, hbm),
-        scratch_shapes=[pltpu.VMEM((slots, steps, all_heads, width), F32), dma((2,))],
-        compiler_params=pltpu.CompilerParams(vmem_limit_bytes=16 * 2**20),
-    )(out, fin, y, gate, gain.reshape(1, -1))
-    return out, dec, fin
+    return pl.pallas_call(
+        finish,
+        out_shape=shapes,
+        in_specs=[hbm] * 3,
+        out_specs=(hbm,) * 3,
+        scratch_shapes=[dma((3,))],
+        compiler_params=pltpu.CompilerParams(vmem_limit_bytes=64 * 2**20),
+    )(*made)
 
 
 def solution(mesh):

time: 29.2 us -> 38.3 us (1.31)
  Pallas kernels: 20.9 us -> 37.4 us
  local copies, waits for them, and re-layouts: 7.04 us -> 0 us
    pallas_call x2, Pallas kernels: 20.9 us -> 37.4 us  [the longest x1 20.3 us: body(): pl.pallas_call(functools.partial(kernel, n_dev, n_sub), out_shape=shapes,...]
    unnamed x24 -> x0, local copies, waits for them, and re-layouts: 7.04 us -> none
where the time goes in v3:
time: 38.3 us; the launch traced here: 38.1 us
  Pallas kernels  37.4 us (98%)
  between operations  0.64 us (2%)
    pallas_call x1, Pallas kernels, body(): pl.pallas_call(functools.partial(kernel, n_dev, n_sub), out_shape=shapes,...  20.3 us
    pallas_call x1, Pallas kernels, body(): pl.pallas_call(finish, out_shape=shapes, in_specs=[hbm] * 3, out_specs=(h...  17.1 us

profile of v3, /device:TPU:0, one launch (start us, length us, event | category | flops | bytes accessed | tf_op | source)
XLA Modules:
  0.0 38.1 jit_solution(4586575917020562463)
XLA Ops:
  0.6 20.3 %shard_map.139 = (bf16[2,2,256,128]{3,2,1,0:T(8,128)(2,1)}, bf16[2,4,256]{2,1,0:T(4,128)(2,1)}, f32[2,8,32,128]{3,2,1,0:T(8,128)}) custom-call(bf16[2,2,256,128]{3,2,1,0:T(8,128)(2,1)} %q_hbm.1, bf16[2,2,256,128]{3,2,1,0:T(8,128)(2,1)} %k_hbm.1, bf16[2,2,256,128]{3,2,1,0:T(8,128)(2,1)} %v_hbm.1, f32[2,2,256]{2,1,0:T(2,128)} %d_hbm.1, s32[8]{0:T(128)} %blocks_ref.1, ...), custom_call_target="tpu_custom_call" | custom-call | tf_op jit(solution)/shard_map/pallas_call | solution.py:451
  20.9 17.1 %shard_map.140 = (bf16[2,2,256,128]{3,2,1,0:T(8,128)(2,1)}, bf16[2,4,256]{2,1,0:T(4,128)(2,1)}, f32[2,8,32,128]{3,2,1,0:T(8,128)}) custom-call(bf16[2,2,256,128]{3,2,1,0:T(8,128)(2,1)} %get-tuple-element.6.refs_0_, bf16[2,4,256]{2,1,0:T(4,128)(2,1)} %get-tuple-element.7.refs_1_, f32[2,8,32,128]{3,2,1,0:T(8,128)} %get-tuple-element.8.refs_2_), custom_call_target="tpu_custom_call" | custom-call | tf_op jit(solution)/shard_map/pallas_call | solution.py:504

commit v4 on v2

--- a/solution.py
+++ b/solution.py
@@ -1,4 +1,5 @@
 import functools
+import math
 
 import jax
 import jax.numpy as jnp
@@ -61,9 +62,12 @@
     kd_hbm,
     vd_hbm,
     dd_hbm,
+    gate_hbm,
+    gain_hbm,
     pbuf,
     fsbuf,
     ybuf,
+    scale_ref,
     q_ref,
     k_ref,
     v_ref,
@@ -72,6 +76,8 @@
     kd_ref,
     vd_ref,
     dd_ref,
+    gate_ref,
+    gain_ref,
     sbuf,
     bbuf,
     rbuf,
@@ -108,6 +114,8 @@
                 (kd_hbm, kd_ref),
                 (qd_hbm, qd_ref),
                 (vd_hbm, vd_ref),
+                (gate_hbm, gate_ref),
+                (gain_hbm, gain_ref),
             )
         )
     ]
@@ -360,6 +368,8 @@
         for j in range(slots):
             decode_ahead(j, c)
     each(0, group, functools.partial(output, heads - 1))
+    for j in range(slots):
+        scale_ref[j] = jax.nn.sigmoid(gate_ref[j].astype(F32)) * gain_ref[...]
 
     for hd in range(heads):
         each(1, n_dev, lambda i: copy_b(hd, i).wait_recv())
@@ -374,7 +384,7 @@
 
 
 def finish(
-    n_sub, out_ref, fin_ref, y_ref, gate_ref, gain_ref, out_hbm, dec_ref, fin_hbm, ysum, sems
+    n_sub, out_ref, fin_ref, y_ref, scale_ref, out_hbm, dec_ref, fin_hbm, ysum, sems
 ):
     saves = [
         pltpu.make_async_copy(out_ref, out_hbm, sems.at[0]),
@@ -399,7 +409,7 @@
             square = square + jnp.sum((y * y).reshape(steps, CHUNK, width), axis=1)
         mean = jnp.sum(square, axis=1, keepdims=True) / (all_heads * width)
         inverse = lax.rsqrt(mean + EPSILON)
-        gates = jax.nn.sigmoid(gate_ref[j].astype(F32)) * gain_ref[...]
+        gates = scale_ref[j]
         for h in range(share):
             y = jnp.concatenate(
                 [ysum[j, s, pl.ds(sub * share + h, 1), :] for s in range(steps)], axis=0
@@ -425,15 +435,18 @@
     turned = (slots, steps, all_heads, rows)
     state = jax.ShapeDtypeStruct((slots, all_heads, rows, width), F32)
     parts = (n_sub, chunks, slots, steps * CHUNK, width)
+    kept = 2 * math.prod(q.shape) + 4 * (math.prod(state.shape) + math.prod(parts))
+    limit = 62 * 2**20 - kept
     made = pl.pallas_call(
         functools.partial(kernel, n_dev, n_sub),
         out_shape=(
-            jax.ShapeDtypeStruct(q.shape, BF16),
-            state,
-            jax.ShapeDtypeStruct(parts, F32),
+            pltpu.VMEM(q.shape, BF16),
+            pltpu.VMEM(state.shape, F32),
+            pltpu.VMEM(parts, F32),
+            pltpu.VMEM((slots, steps, gain.shape[0]), F32),
         ),
-        in_specs=[hbm] * 4 + [smem] * 2 + [hbm] * 4,
-        out_specs=(vmem, vmem, vmem),
+        in_specs=[hbm] * 4 + [smem] * 2 + [hbm] * 6,
+        out_specs=(vmem, vmem, vmem, vmem),
         scratch_shapes=[
             pltpu.VMEM(q.shape, BF16),
             pltpu.VMEM(q.shape, BF16),
@@ -443,6 +456,8 @@
             pltpu.VMEM(turned, BF16),
             pltpu.VMEM(vd.shape, BF16),
             pltpu.VMEM(dd.shape, F32),
+            pltpu.VMEM(gate.shape, BF16),
+            pltpu.VMEM((1, gain.shape[0]), F32),
             pltpu.VMEM((heads, n_sub, group, rows, width), F32),
             pltpu.VMEM((heads, n_dev, slots, rows, width), F32),
             pltpu.VMEM((n_dev, heads, slots, rows, width), F32),
@@ -455,11 +470,11 @@
             dma((heads, n_dev)),
             dma((n_sub,)),
             dma((n_sub,)),
-            dma((8,)),
+            dma((10,)),
         ]
         + [pltpu.VMEM((requests, rows, width), F32)] * heads,
         compiler_params=pltpu.CompilerParams(
-            collective_id=0, has_side_effects=True, vmem_limit_bytes=40 * 2**20
+            collective_id=0, has_side_effects=True, vmem_limit_bytes=limit
         ),
     )(
         q,
@@ -472,8 +487,9 @@
         jnp.swapaxes(kd, 2, 3),
         vd,
         dd,
+        gate,
+        gain.reshape(1, -1),
     )
-    out, fin, y = made
     out, dec, fin = pl.pallas_call(
         functools.partial(finish, n_sub),
         out_shape=(
@@ -481,11 +497,11 @@
             jax.ShapeDtypeStruct(gate.shape, BF16),
             state,
         ),
-        in_specs=[pl.BlockSpec(memory_space=pl.ANY)] * 2 + [vmem] * 3,
+        in_specs=[vmem] * 4,
         out_specs=(hbm, vmem, hbm),
         scratch_shapes=[pltpu.VMEM((slots, steps, all_heads, width), F32), dma((2,))],
         compiler_params=pltpu.CompilerParams(vmem_limit_bytes=16 * 2**20),
-    )(out, fin, y, gate, gain.reshape(1, -1))
+    )(*made)
     return out, dec, fin
 
 

time: 29.2 us -> 21.8 us (0.75); the launches traced: 28.7 us -> 21.6 us
  local copies, waits for them, and re-layouts: 7.04 us -> 0 us
    unnamed x24 -> x0, local copies, waits for them, and re-layouts: 7.04 us -> none
where the time goes in v4:
time: 21.8 us; the launch traced here: 21.6 us
  Pallas kernels  21 us (96%)
  between operations  0.64 us (3%)
    pallas_call x1, Pallas kernels, body(): pl.pallas_call(functools.partial(kernel, n_dev, n_sub), out_shape=(pltpu....  19.6 us
    pallas_call x1, Pallas kernels, body(): pl.pallas_call(functools.partial(finish, n_sub), out_shape=(jax.ShapeDtyp...  1.41 us

profile of v4, /device:TPU:0, one launch (start us, length us, event | category | flops | bytes accessed | tf_op | source)
XLA Modules:
  0.0 21.6 jit_solution(15435792114135699821)
XLA Ops:
  0.6 19.6 %shard_map.139 = (bf16[2,2,256,128]{3,2,1,0:T(8,128)(2,1)S(1)}, f32[2,8,32,128]{3,2,1,0:T(8,128)S(1)}, f32[4,1,2,32,128]{4,3,2,1,0:T(8,128)S(1)}, f32[2,4,256]{2,1,0:T(4,128)S(1)}) custom-call(bf16[2,2,256,128]{3,2,1,0:T(8,128)(2,1)} %q_hbm.1, bf16[2,2,256,128]{3,2,1,0:T(8,128)(2,1)} %k_hbm.1, bf16[2,2,256,128]{3,2,1,0:T(8,128)(2,1)} %v_hbm.1, ...), custom_call_target="tpu_custom_call" | custom-call | tf_op jit(solution)/shard_map/pallas_call | solution.py:440
  20.2 1.4 %shard_map.140 = (bf16[2,2,256,128]{3,2,1,0:T(8,128)(2,1)}, bf16[2,4,256]{2,1,0:T(4,128)(2,1)}, f32[2,8,32,128]{3,2,1,0:T(8,128)}) custom-call(bf16[2,2,256,128]{3,2,1,0:T(8,128)(2,1)S(1)} %get-tuple-element.7.out_ref, f32[2,8,32,128]{3,2,1,0:T(8,128)S(1)} %get-tuple-element.8.fin_ref, f32[4,1,2,32,128]{4,3,2,1,0:T(8,128)S(1)} %get-tuple-element.9.y_ref, ...), custom_call_target="tpu_custom_call" | custom-call | tf_op jit(solution)/shard_map/pallas_call | solution.py:493
